TPU v7x, 256 devices: a whole 4x4x8 slice. The times are simulated.
256 devices in a mesh: section: 8 (over z_lo, core), dp: 4 (over x), mp: 8 (over z_hi, y).
Axes of the slice: x: 4, y: 4, z: 8 (z_hi: 2, z_lo: 4; z = z_hi * 4 + z_lo), core: 2. Of those that a mesh axis runs over, the one named last changes fastest.
Arguments:
- taps: bfloat16 [4, 16, 64, 64, 4096], P(None, 'dp', 'mp', None, 'section'), may hold values from -6 to 6
- ln_gain: float32 [4, 4096], P(None, 'section'), may hold values from 0.1 to 1.9
- w_proj: bfloat16 [4, 4096, 256], P(None, ('section', 'dp', 'mp')), may hold values from -0.09375 to 0.09375
- conv_one: bfloat16 [2304, 256], P(('dp', 'mp')), may hold values from -0.125 to 0.125
- conv_two: bfloat16 [2304, 256], P(('dp', 'mp'), 'section'), may hold values from -0.125 to 0.125
Outputs:
- refined: bfloat16 [16, 64, 64, 256], P('dp', 'mp', None, 'section')
All inputs are finite; a program needn't handle non-finite values.
Results may differ from a plain program's by a relative error of at most 0.023.
Values may be sent and summed in bfloat16 or wider, within the bound.
A program may use at most 128 MiB of HBM per device.

v0:
```python
import jax
import jax.numpy as jnp
from jax import lax
from jax.sharding import PartitionSpec as P

D = 4096


def extended(x, sides, width):
    for axis, dim in sides:
        peers, length = (lax.axis_size(axis), x.shape[dim])
        up = [(i, (i + 1) % peers) for i in range(peers - 1)]
        down = [(j, i) for i, j in up]
        last = lax.slice_in_dim(x, length - width, length, axis=dim)
        leading = lax.slice_in_dim(x, 0, width, axis=dim)
        before = lax.ppermute(last, axis, up)
        after = lax.ppermute(leading, axis, down)
        x = jnp.concatenate([before, x, after], axis=dim)
    return x


def patches(act):
    widened = extended(act, (("mp", 1),), 1)
    padded = jnp.pad(widened, ((0, 0), (0, 0), (1, 1), (0, 0)))
    height = act.shape[1]
    width = act.shape[2]
    columns = jnp.concatenate(
        [padded[:, a : a + height, b : b + width, :] for a in range(3) for b in range(3)], axis=-1
    )
    return columns.reshape(-1, columns.shape[-1])


def folder(columns, piece):
    return jnp.dot(columns, piece, preferred_element_type=jnp.float32)


def first_conv(act, weight):
    columns = patches(act)
    result = folder(columns, lax.all_gather(weight, ("dp", "mp"), axis=0, tiled=True))
    return result.reshape(act.shape[0], act.shape[1], act.shape[2], weight.shape[1])


def second_conv(act, weight):
    columns = patches(act)
    result = folder(columns, lax.all_gather(weight, ("dp", "mp"), axis=0, tiled=True))
    return result.reshape(act.shape[0], act.shape[1], act.shape[2], weight.shape[1])


def per_device(taps, ln_gain, w_proj, conv_one, conv_two):
    layers, images, rows, cols, feat_share = taps.shape
    channels = w_proj.shape[2]
    values = taps.astype(jnp.float32).reshape(layers, -1, feat_share)
    sums_local = jnp.sum(values, axis=-1, keepdims=True)
    squares_local = jnp.sum(values * values, axis=-1, keepdims=True)
    sums_all, squares_all = (
        lax.psum(sums_local.astype(jnp.bfloat16), "section").astype(jnp.float32),
        lax.psum(squares_local.astype(jnp.bfloat16), "section").astype(jnp.float32),
    )
    center = sums_all / D
    deviation = jnp.maximum(squares_all / D - center * center, 0.0)
    normed = ((values - center) * lax.rsqrt(deviation + 1e-06) * ln_gain[:, None, :]).astype(
        jnp.bfloat16
    )
    partial_sum = jnp.einsum(
        "tnk,tkc->nc",
        normed,
        lax.all_gather(w_proj, ("dp", "mp"), axis=1, tiled=True),
        preferred_element_type=jnp.float32,
    ).reshape(images, rows, cols, channels)
    share = channels // lax.axis_size("section")
    offset = lax.axis_index("section") * share
    joined = lax.psum(partial_sum.astype(jnp.bfloat16), "section").astype(jnp.float32)
    act_one = jnp.maximum(joined, 0.0).astype(jnp.bfloat16)
    act_two = jnp.maximum(first_conv(act_one, conv_one), 0.0).astype(jnp.bfloat16)
    kept = lax.dynamic_slice_in_dim(joined, offset, share, 3)
    return (kept + second_conv(act_two, conv_two)).astype(jnp.bfloat16)


def solution(mesh):
    placed = (
        P(None, "dp", "mp", None, "section"),
        P(None, "section"),
        P(None, ("section", "dp", "mp"), None),
        P(("dp", "mp"), None),
        P(("dp", "mp"), "section"),
    )
    return jax.shard_map(
        per_device,
        mesh=mesh,
        in_specs=placed,
        out_specs=P("dp", "mp", None, "section"),
        check_vma=False,
    )
```

profile of v0, /device:TPU:8, one launch (start us, length us, event | category | flops | bytes accessed | tf_op | source)
XLA Modules:
  0.0 419.2 jit_solution(7747318474145401546)
XLA Ops:
  7.3 4.6 %reduce_sum.21 = bf16[4,4,8,64]{3,2,1,0:T(8,128)(2,1)S(1)} reduce(bf16[4,4,8,64,512]{4,3,2,1,0:T(8,128)(2,1)} %param.5, bf16[]{:T(256)} %constant.9.clone.1), dimensions={4}, to_apply=%region_0.0 | reduce | flops 4186112 | bytes 8404994 | tf_op jit(solution)/shard_map/reduce_sum | solution.py:53
  12.0 5.1 %multiply_reduce_fusion = bf16[4,4,8,64]{3,2,1,0:T(8,128)(2,1)S(1)} fusion(bf16[4,4,8,64,512]{4,3,2,1,0:T(8,128)(2,1)} %param.5), kind=kLoop, calls=%fused_computation.4 | loop fusion | flops 12574720 | bytes 8404992 | tf_op jit(solution)/shard_map/reduce_sum | solution.py:54
  17.2 30.3 %all-reduce.2 = (bf16[4,2048,1]{1,0,2:T(4,128)(2,1)S(1)}, bf16[4,2048,1]{1,0,2:T(4,128)(2,1)S(1)}) all-reduce(bf16[4,2048,1]{1,0,2:T(4,128)(2,1)S(1)} %convert_element_type.60, bf16[4,2048,1]{1,0,2:T(4,128)(2,1)S(1)} %convert_element_type.57), channel_id=1, replica_groups=mesh['section'=8,'dp'=4,'mp'=8] {'section'}, use_global_device_ids=true, to_apply=%region_3.0 | all-reduce | flops 16384 | bytes 65536 | tf_op jit(solution)/shard_map/psum | solution.py:57
  47.5 8.3 %fusion.2 = bf16[4,2048,512]{2,1,0:T(8,128)(2,1)} fusion(f32[4,512]{1,0:T(4,128)S(1)} %copy-done.1, f32[4,2048]{1,0:T(4,128)S(1)} %get-tuple-element.14, f32[4,2048]{1,0:T(4,128)S(1)} %get-tuple-element.13, bf16[4,4,8,64,512]{4,3,2,1,0:T(8,128)(2,1)} %param.5), kind=kLoop, calls=%fused_computation.3 | loop fusion | flops 20971520 | bytes 16850944 | tf_op jit(solution)/shard_map/convert_element_type | solution.py:61
  55.8 38.7 %all-gather.4.cloned.1.call-done = bf16[4,512,256]{2,1,0:T(8,128)(2,1)} async-done(((bf16[4,16,256]{2,1,0:T(8,128)(2,1)}), bf16[4,512,256]{2,1,0:T(8,128)(2,1)}) %all-gather.4.cloned.1.call-update) | async-done | bytes 1048592 | tf_op jit(solution)/shard_map/all_gather | solution.py:67
  94.5 7.3 %fusion.11 = bf16[4,8,64,256]{2,3,0,1:T(8,128)(2,1)S(1)} fusion(bf16[4,8,64,512,4]{3,2,1,0,4:T(8,128)(2,1)} %bitcast.39, bf16[4,512,256]{2,1,0:T(8,128)(2,1)} %all-gather.4.cloned.1.call-done), kind=kOutput, calls=%fused_computation.20 | convolution fusion | flops 2147483648 | bytes 10485760 | tf_op jit(solution)/shard_map/tnk,tkc->nc/dot_general | solution.py:64
  103.3 75.4 %all-reduce.5.cloned.1.call-done = bf16[4,8,64,256]{2,3,1,0:T(8,128)(2,1)} async-done(((bf16[4,8,64,256]{2,3,1,0:T(8,128)(2,1)}), bf16[4,8,64,256]{2,3,1,0:T(8,128)(2,1)}) %all-reduce.5.cloned.1.call-update) | async-done | bytes 1048592 | tf_op jit(solution)/shard_map/psum | solution.py:72
  178.7 2.2 maximum_convert_fusion.1
  180.9 3.4 collective-permute-start
  184.3 2.6 collective-permute-start.1
  187.0 2.7 collective-permute-done
  189.7 3.1 collective-permute-done.1
  196.4 1.9 fusion.17
  198.3 2.1 slice_dynamic-update-slice_fusion.10
  202.1 3.4 fusion.23
  205.5 2.0 slice_dynamic-update-slice_fusion.8
  211.1 2.0 slice_dynamic-update-slice_fusion.6
  213.1 59.1 %all-gather.6.cloned.1.call-done = bf16[2304,256]{1,0:T(8,128)(2,1)} async-done(((bf16[72,256]{1,0:T(8,128)(2,1)}), bf16[2304,256]{1,0:T(8,128)(2,1)}) %all-gather.6.cloned.1.call-update) | async-done | bytes 1179664 | tf_op jit(solution)/shard_map/all_gather | solution.py:39
  272.2 9.4 %maximum_convert_fusion = bf16[4,8,64,256]{2,3,1,0:T(8,128)(2,1)S(1)} fusion(bf16[4,8,64,2304]{2,3,1,0:T(8,128)(2,1)} %slice_dynamic-update-slice_fusion.6, bf16[2304,256]{1,0:T(8,128)(2,1)} %all-gather.6.cloned.1.call-done), kind=kOutput, calls=%fused_computation.11 | convolution fusion | flops 2416967680 | bytes 11665408 | tf_op jit(solution)/shard_map/dot_general | solution.py:34
  281.6 3.1 collective-permute-start.2
  284.7 2.7 collective-permute-start.3
  287.5 111.4 %all-gather = bf16[32,72,32]{1,2,0:T(8,128)(2,1)S(1)} all-gather(bf16[1,72,32]{1,2,0:T(8,128)(2,1)S(1)} %bitcast.40), channel_id=1, replica_groups=mesh['section'=8,'dp'=4,'mp'=8] {'dp','mp'}, dimensions={0}, use_global_device_ids=true | all-gather | bytes 152064 | tf_op jit(solution)/shard_map/all_gather | solution.py:45
  399.3 1.9 select_maximum_fusion
  407.6 5.1 %fusion.18 = bf16[4,8,64,32]{2,3,1,0:T(8,128)(2,1)} fusion(bf16[4,8,64,2304]{2,3,1,0:T(8,128)(2,1)S(1)} %slice_dynamic-update-slice_fusion, f32[4,8,64,256]{2,3,1,0:T(8,128)} %get-tuple-element.7, s32[]{:T(128)S(6)} %select_n.3, bf16[2304,32,1,1]{0,1,2,3:T(8,128)(2,1)S(1)} %reshape.48), kind=kOutput, calls=%fused_computation.42 | convolution fusion | flops 302120960 | bytes 9977860 | tf_op jit(solution)/shard_map/dot_general | solution.py:34
  (36 shorter events, 18.3 us)
Async XLA Ops:
  6.5 88.0 %all-gather.4.cloned.1.call-start = ((), (), s32[]{:S(2)}) async-start(), calls=%async_computation | async-start | bytes 1081344 | tf_op jit(solution)/shard_map/all_gather | solution.py:67
  7.3 171.4 %all-reduce.5.cloned.1.call-start = ((), (), s32[]{:S(2)}) async-start(), calls=%async_computation.1 | async-start | bytes 4194304 | tf_op jit(solution)/shard_map/psum | solution.py:72
  12.0 35.5 %copy-start.1 = (f32[4,512]{1,0:T(4,128)S(1)}, f32[4,512]{1,0:T(4,128)}, u32[]{:S(2)}) copy-start(f32[4,512]{1,0:T(4,128)} %param.6) | copy-start | bytes 24580
  103.3 168.9 %all-gather.6.cloned.1.call-start = ((), (), s32[]{:S(2)}) async-start(), calls=%async_computation.2 | async-start | bytes 1216512 | tf_op jit(solution)/shard_map/all_gather | solution.py:39
  180.9 8.7 %collective-permute-start = (bf16[4,1,64,256]{2,3,1,0:T(8,128)(2,1)S(1)}, bf16[4,1,64,256]{2,3,1,0:T(8,128)(2,1)S(1)}, u32[]{:S(2)}, u32[]{:S(2)}) collective-permute-start(bf16[4,1,64,256]{2,3,1,0:T(8,128)(2,1)S(1)} %get-tuple-element.11), channel_id=1, source_target_pairs={{0,1},{1,2},{2,3},{3,4},{4,5},{5,6},{6,7},{8,9},{9,10},{10,11},{11... | collective-permute-start | bytes 393224 | tf_op jit(solution)/shard_map/ppermute | solution.py:16
  184.3 8.5 %collective-permute-start.1 = (bf16[4,1,64,256]{2,3,1,0:T(8,128)(2,1)S(1)}, bf16[4,1,64,256]{2,3,1,0:T(8,128)(2,1)S(1)}, u32[]{:S(2)}, u32[]{:S(2)}) collective-permute-start(bf16[4,1,64,256]{2,3,1,0:T(8,128)(2,1)S(1)} %get-tuple-element.12), channel_id=1, source_target_pairs={{1,0},{2,1},{3,2},{4,3},{5,4},{6,5},{7,6},{9,8},{10,9},{11,10},{12... | collective-permute-start | bytes 393224 | tf_op jit(solution)/shard_map/ppermute | solution.py:17
  198.3 3.8 copy-start
  213.1 74.4 %copy-start.2 = (bf16[72,32]{0,1:T(8,128)(2,1)S(1)}, bf16[72,32]{0,1:T(8,128)(2,1)}, u32[]{:S(2)}) copy-start(bf16[72,32]{0,1:T(8,128)(2,1)} %param.9) | copy-start | bytes 13828
  281.6 117.7 %collective-permute-start.2 = (bf16[4,1,64,256]{2,3,1,0:T(8,128)(2,1)S(1)}, bf16[4,1,64,256]{2,3,1,0:T(8,128)(2,1)S(1)}, u32[]{:S(2)}, u32[]{:S(2)}) collective-permute-start(bf16[4,1,64,256]{2,3,1,0:T(8,128)(2,1)S(1)} %get-tuple-element.9), channel_id=1, source_target_pairs={{0,1},{1,2},{2,3},{3,4},{4,5},{5,6},{6,7},{8,9},{9,10},{10,11},{11... | collective-permute-start | bytes 393224 | tf_op jit(solution)/shard_map/ppermute | solution.py:16
  284.7 114.6 %collective-permute-start.3 = (bf16[4,1,64,256]{2,3,1,0:T(8,128)(2,1)S(1)}, bf16[4,1,64,256]{2,3,1,0:T(8,128)(2,1)S(1)}, u32[]{:S(2)}, u32[]{:S(2)}) collective-permute-start(bf16[4,1,64,256]{2,3,1,0:T(8,128)(2,1)S(1)} %get-tuple-element.10), channel_id=1, source_target_pairs={{1,0},{2,1},{3,2},{4,3},{5,4},{6,5},{7,6},{9,8},{10,9},{11,10},{12... | collective-permute-start | bytes 393224 | tf_op jit(solution)/shard_map/ppermute | solution.py:17
Sparse Core Ops, SparseCore 0:
  10.6 83.8 all-gather.3
  103.4 75.2 all-reduce.4
  187.1 85.0 all-gather.5
where the time goes:
time: 420 us; the launch traced here: 419 us
  waiting for transfers between devices  180 us (43%)
  blocking collectives  142 us (34%)
  other arithmetic  32.6 us (8%)
  matrix products  21.7 us (5%)
  local copies, waits for them, and re-layouts  18.3 us (4%)
  between operations  13.3 us (3%)
  starting transfers between devices  12 us (3%)
    all_gather x1, blocking collectives, second_conv(): lax.all_gather(weight, ('dp', 'mp'), axis=0, tiled=True)  111 us
    psum x1, waiting for transfers between devices, per_device(): lax.psum(partial_sum.astype(jnp.bfloat16), 'section').astype(jnp.float32)  75.4 us
    all_gather x1, waiting for transfers between devices, first_conv(): lax.all_gather(weight, ('dp', 'mp'), axis=0, tiled=True)  59.1 us
    all_gather x1, waiting for transfers between devices, per_device(): lax.all_gather(w_proj, ('dp', 'mp'), axis=1, tiled=True)  38.7 us
    psum x1, blocking collectives, per_device(): lax.psum(squares_local.astype(jnp.bfloat16), 'section').astype(jnp.float32)  30.3 us
    dot_general x2, matrix products, folder(): return jnp.dot(columns, piece, preferred_element_type=jnp.float32)  14.5 us
    unnamed x18, local copies, waits for them, and re-layouts  13.1 us
  transfers between devices with their start and end apart: 7, of which 5 were waited for; matrix products, arithmetic and copies ran while one was open for 9% of the time, Pallas kernels for 0%

commit v1 on v0

v1 whole, which is shorter than its diff:
```python
import jax
import jax.numpy as jnp
from jax import lax
from jax.experimental import pallas as pl
from jax.experimental.pallas import tpu as pltpu
from jax.sharding import PartitionSpec as P

D = 4096
TAPS = 4
MESH = pl.DeviceIdType.MESH
F32 = jnp.float32
BF16 = jnp.bfloat16


class Links:
    def __init__(self, send_sems, recv_sems):
        self.send_sems, self.recv_sems = send_sems, recv_sems
        self.used = 0
        self.copies = []

    def start(self, src, dst, to):
        copy = pltpu.make_async_remote_copy(
            src_ref=src,
            dst_ref=dst,
            send_sem=self.send_sems.at[self.used],
            recv_sem=self.recv_sems.at[self.used],
            device_id=to,
            device_id_type=MESH,
        )
        self.used += 1
        copy.start()
        self.copies.append(copy)
        return copy

    def finish(self):
        for copy in self.copies:
            copy.wait_send()


N_COPIES = 96


def kernel(
    taps_hbm, gain_ref, w_ref, c1_ref, c2_ref, out_ref,
    taps, part, wall, gw, gsum, gcol, c2pad, c2all, piece, call_, conv, tot, tparts, tred, tall, tcols,
    joint, jsib, jsum, jrecv, act, hsib, hcross, x1, x2, res, packed,
    tap_sems, send_sems, recv_sems,
):
    sec, x, mp = lax.axis_index("section"), lax.axis_index("dp"), lax.axis_index("mp")
    zlo, core = sec // 2, sec % 2
    zhi, y = mp // 4, mp % 4
    links = Links(send_sems, recv_sems)

    reads = [pltpu.make_async_copy(taps_hbm.at[t], taps.at[t], tap_sems.at[t]) for t in range(TAPS)]
    for read in reads:
        read.start()

    peers = [{"section": (sec + k) % 8} for k in range(1, 8)]
    x_up, x_down = {"dp": (x + 1) % 4}, {"dp": (x + 3) % 4}
    y_up, y_down = {"mp": zhi * 4 + (y + 1) % 4}, {"mp": zhi * 4 + (y + 3) % 4}
    z_far = {"mp": (1 - zhi) * 4 + y}
    cross = {"mp": (mp + 7 + 2 * core) % 8, "section": zlo * 2 + 1 - core}
    sibling = {"section": zlo * 2 + 1 - core}

    barrier = pltpu.get_barrier_semaphore()
    greeted = peers + [x_up, x_down, y_up, y_down, z_far, cross]
    for device in greeted:
        pl.semaphore_signal(barrier, inc=1, device_id=device, device_id_type=MESH)

    c2pad[...] = jnp.zeros_like(c2pad)
    c2pad[0:72, 0:32] = c2_ref[...]
    for t in range(TAPS):
        wall[t, x, zhi, y] = w_ref[t]
    pl.semaphore_wait(barrier, len(greeted))

    w_far = links.start(wall.at[:, x, zhi, y], wall.at[:, x, zhi, y], z_far)
    c2_got = [links.start(c2pad, c2all.at[k], peers[k - 1]) for k in range(1, 8)]

    lane = lax.broadcasted_iota(jnp.int32, (128, 128), 1)

    def stats(t, total):
        def body(b, total):
            v = taps[t, pl.ds(pl.multiple_of(b * 128, 128), 128), :].astype(F32)
            s = jnp.sum(v, axis=1, keepdims=True)
            q = jnp.sum(v * v, axis=1, keepdims=True)
            total = jnp.where(lane == b * 8 + t, s, total)
            return jnp.where(lane == b * 8 + 4 + t, q, total)

        return lax.fori_loop(0, 16, body, total)

    def w_first(part_, i, j):
        return wall.at[part_, i, :, j]

    class Spread:
        def __init__(self, view):
            self.view = view

        def begin(self):
            v = self.view
            a, b = v(0, None, x, y), v(1, None, x, y)
            self.a1, self.a2 = links.start(a, a, x_up), links.start(a, a, x_down)
            self.b1, self.b2 = links.start(b, b, y_up), links.start(b, b, y_down)

        def forward(self):
            v = self.view
            xm, xp, ym, yp = (x + 3) % 4, (x + 1) % 4, (y + 3) % 4, (y + 1) % 4
            self.a1.wait_recv()
            s = v(0, 0, xm, y)
            self.a3 = links.start(s, s, x_up)
            self.a2.wait_recv()
            s = v(0, 1, xp, y)
            self.a4 = links.start(s, s, x_down)
            self.b1.wait_recv()
            s = v(1, 0, x, ym)
            self.b3 = links.start(s, s, y_up)
            self.b2.wait_recv()
            s = v(1, 1, x, yp)
            self.b4 = links.start(s, s, y_down)

        def begin_second(self):
            v = self.view
            every = slice(None)
            self.a3.wait_recv()
            self.a4.wait_recv()
            a = v(0, None, every, y)
            self.a1, self.a2 = links.start(a, a, y_up), links.start(a, a, y_down)
            self.b3.wait_recv()
            self.b4.wait_recv()
            b = v(1, None, x, every)
            self.b1, self.b2 = links.start(b, b, x_up), links.start(b, b, x_down)

        def forward_second(self):
            v = self.view
            every = slice(None)
            xm, xp, ym, yp = (x + 3) % 4, (x + 1) % 4, (y + 3) % 4, (y + 1) % 4
            self.a1.wait_recv()
            s = v(0, 0, every, ym)
            self.a3 = links.start(s, s, y_up)
            self.a2.wait_recv()
            s = v(0, 1, every, yp)
            self.a4 = links.start(s, s, y_down)
            self.b1.wait_recv()
            s = v(1, 0, xm, every)
            self.b3 = links.start(s, s, x_up)
            self.b2.wait_recv()
            s = v(1, 1, xp, every)
            self.b4 = links.start(s, s, x_down)

        def finish(self):
            for copy in (self.a3, self.a4, self.b3, self.b4):
                copy.wait_recv()

    w_rows = {(0, None): slice(0, 2), (0, 0): slice(0, 1), (0, 1): slice(1, 2),
              (1, None): slice(2, 4), (1, 0): slice(2, 3), (1, 1): slice(3, 4)}
    c_rows = {(0, None): slice(0, 48), (0, 0): slice(0, 32), (0, 1): slice(32, 48),
              (1, None): slice(48, 80), (1, 0): slice(48, 64), (1, 1): slice(64, 80)}
    w_spread = Spread(lambda half, which, xs, ys: wall.at[w_rows[half, which], xs, :, ys])
    c_spread = Spread(lambda half, which, xs, ys: call_.at[core, xs, :, ys, c_rows[half, which]])

    reads[0].wait()
    total = stats(0, jnp.zeros((128, 128), F32))
    w_far.wait_recv()
    w_spread.begin()

    for copy in c2_got:
        copy.wait_recv()
    left, right = jnp.zeros((80, 128), F32), jnp.zeros((80, 128), F32)
    c2all[0] = c2pad[...]
    for d in range(8):
        block = c2all[(sec - d + 8) % 8].astype(F32)
        block = pltpu.roll(block, 32 * (d % 4), 1) if d % 4 else block
        if d < 4:
            left = left + block
        else:
            right = right + block
    first = jnp.concatenate([c1_ref[...].astype(F32), jnp.zeros((8, 256), F32)], axis=0)
    second = jnp.concatenate([left, right], axis=1)
    call_[core, x, zhi, y] = jnp.where(core == 0, first, second).astype(BF16)
    mine = call_.at[core, x, zhi, y]
    c_far = links.start(mine, mine, z_far)

    reads[1].wait()
    total = stats(1, total)
    w_spread.forward()
    reads[2].wait()
    total = stats(2, total)
    w_spread.begin_second()
    reads[3].wait()
    total = stats(3, total)
    tot[...] = total.T.reshape(8, 16, 128)
    sent = [links.start(tot.at[(sec + k) % 8], tparts.at[k], peers[k - 1]) for k in range(1, 8)]
    w_spread.forward_second()

    gcol[...] = jnp.zeros_like(gcol)
    gcol[0:4, :] = gain_ref[...]
    gains = gcol[...].T

    mine = tot[sec]
    for k in range(1, 8):
        sent[k - 1].wait_recv()
        mine = mine + tparts[k]
    outs = []
    for blk in range(2):
        mean = mine[8 * blk : 8 * blk + 4] / D
        var = jnp.maximum(mine[8 * blk + 4 : 8 * blk + 8] / D - mean * mean, 0.0)
        r = lax.rsqrt(var + 1e-6)
        outs += [r, r * mean]
    tall[sec] = jnp.concatenate(outs, axis=0)
    mine = tall.at[sec]
    sent = [links.start(mine, mine, peers[k - 1]) for k in range(1, 8)]

    c_far.wait_recv()
    c_spread.begin()
    w_spread.finish()

    for t in range(TAPS):
        scaled = (wall[t].reshape(512, 256).astype(F32) * gains[:, t : t + 1]).astype(BF16)
        gw[t] = scaled
        gsum[t] = jnp.sum(scaled.astype(F32), axis=0, keepdims=True)

        def project(i, _, t=t):
            rows = pl.ds(pl.multiple_of(i * 512, 512), 512)
            part[t, rows, :] = jnp.dot(taps[t, rows, :], gw[t], preferred_element_type=F32)
            return 0

        lax.fori_loop(0, 4, project, 0)
    c_spread.forward()

    for copy in sent:
        copy.wait_recv()
    tcols[...] = tall[...].reshape(128, 128).T

    def combine(b):
        cols = pltpu.roll(tcols[...], (128 - 8 * b) % 128, 1)
        rows = pl.ds(pl.multiple_of(b * 128, 128), 128)
        acc = cols[:, 0:1] * part[0, rows, :] - cols[:, 4:5] * gsum[0]
        for t in range(1, TAPS):
            acc = acc + (cols[:, t : t + 1] * part[t, rows, :] - cols[:, 4 + t : 5 + t] * gsum[t])
        return acc.astype(BF16)

    swaps = {}
    z_sent = {}

    def reduce(k):
        image = (zlo + k) % 4
        swaps[k].wait_recv()
        jsum[k] = (joint[image, core].astype(F32) + jsib[k].astype(F32)).astype(BF16)
        z_sent[k] = links.start(jsum.at[k], jrecv.at[k], {"section": (sec + 2 * k) % 8})

    for k in (1, 2, 3, 0):
        image = (zlo + k) % 4

        def strip(h, _, image=image):
            half = lax.rem(h + 1 - core + 2, 2)
            for blk in range(2):
                joint[image, half, blk * 128 : blk * 128 + 128] = combine(image * 4 + half * 2 + blk)
            return 0

        lax.fori_loop(0, 2, strip, 0)
        swaps[k] = links.start(joint.at[image, 1 - core], jsib.at[k], sibling)
        if k == 2:
            reduce(1)
        if k == 3:
            reduce(2)
        if k == 0:
            reduce(3)
    c_spread.begin_second()
    swaps[0].wait_recv()
    own = joint[zlo, core].astype(F32) + jsib[0].astype(F32)
    for k in range(1, 4):
        z_sent[k].wait_recv()
        own = own + jrecv[k].astype(F32)
    res[...] = own
    act[...] = jnp.maximum(own, 0.0).astype(BF16).reshape(2, 128, 256)
    h1 = links.start(act.at[1 - core], hsib, sibling)
    h2 = links.start(act.at[core], hcross, cross)
    c_spread.forward_second()
    c_spread.finish()
    whole = call_.at[core]
    c_swap = links.start(whole, whole, sibling)
    h1.wait_recv()
    h2.wait_recv()

    def columns(value, x_ref, rows):
        col = lax.broadcasted_iota(jnp.int32, (rows, 256), 0) % 64
        x_ref[:, 0:256] = jnp.where(col == 0, 0.0, pltpu.roll(value, 1, 0)).astype(BF16)
        x_ref[:, 256:512] = value.astype(BF16)
        x_ref[:, 512:768] = jnp.where(col == 63, 0.0, pltpu.roll(value, rows - 1, 0)).astype(BF16)

    top = jnp.logical_and(mp == 0, core == 0)
    bottom = jnp.logical_and(mp == 7, core == 1)
    near, far = hsib[...].astype(F32), hcross[...].astype(F32)
    above = jnp.where(core == 0, jnp.where(top, 0.0, far), near)
    below = jnp.where(core == 0, near, jnp.where(bottom, 0.0, far))
    columns(jnp.concatenate([above, jnp.maximum(res[...], 0.0), below], axis=0), x1, 512)

    c_swap.wait_recv()

    def unpack(which):
        def body(p, _):
            i, j, l = p // 4, (p // 2) % 2, 2 * (p % 2)
            one = call_[which, i, j, l].astype(F32)[0:72]
            two = call_[which, i, j, l + 1].astype(F32)[0:72]
            conv[which, pl.ds(pl.multiple_of(p * 144, 16), 144), :] = jnp.concatenate([one, two], axis=0).astype(BF16)
            return 0

        lax.fori_loop(0, 16, body, 0)

    unpack(0)
    mid = jnp.dot(x1[0:384], conv[0, 0:768], preferred_element_type=F32)
    mid = mid + jnp.dot(x1[64:448], conv[0, 768:1536], preferred_element_type=F32)
    mid = mid + jnp.dot(x1[128:512], conv[0, 1536:2304], preferred_element_type=F32)
    row = lax.broadcasted_iota(jnp.int32, (384, 256), 0)
    outside = jnp.logical_or(jnp.logical_and(top, row < 64), jnp.logical_and(bottom, row >= 320))
    columns(jnp.where(outside, 0.0, jnp.maximum(mid, 0.0)), x2, 384)
    unpack(1)
    fin = res[...] + jnp.dot(x2[0:256], conv[1, 0:768], preferred_element_type=F32)
    fin = fin + jnp.dot(x2[64:320], conv[1, 768:1536], preferred_element_type=F32)
    fin = fin + jnp.dot(x2[128:384], conv[1, 1536:2304], preferred_element_type=F32)

    group = lax.broadcasted_iota(jnp.int32, (64, 128), 1) // 32
    for d in range(8):
        got = jnp.zeros((64, 128), F32)
        for g in range(4):
            block = fin[64 * g : 64 * g + 64, 128 * (d // 4) : 128 * (d // 4) + 128]
            turn = (32 * (g - d % 4)) % 128
            block = pltpu.roll(block, turn, 1) if turn else block
            got = jnp.where(group == g, block, got)
        packed[d] = got.astype(BF16)
    outs = [links.start(packed.at[(sec + k) % 8], out_ref.at[sec], peers[k - 1]) for k in range(1, 8)]
    out_ref[sec] = packed[sec]
    for copy in outs:
        copy.wait_recv()
    links.finish()


def per_device(taps, ln_gain, w_proj, conv_one, conv_two):
    vmem = pl.BlockSpec(memory_space=pltpu.VMEM)
    out = pl.pallas_call(
        kernel,
        out_shape=jax.ShapeDtypeStruct((8, 64, 128), BF16),
        in_specs=[pl.BlockSpec(memory_space=pl.ANY)] + [vmem] * 4,
        out_specs=vmem,
        scratch_shapes=[
            pltpu.VMEM((4, 2048, 512), BF16),
            pltpu.VMEM((4, 2048, 256), F32),
            pltpu.VMEM((4, 4, 2, 4, 16, 256), BF16),
            pltpu.VMEM((4, 512, 256), BF16),
            pltpu.VMEM((4, 1, 256), F32),
            pltpu.VMEM((128, 512), F32),
            pltpu.VMEM((80, 128), BF16),
            pltpu.VMEM((8, 80, 128), BF16),
            pltpu.VMEM((80, 256), BF16),
            pltpu.VMEM((2, 4, 2, 4, 80, 256), BF16),
            pltpu.VMEM((2, 2304, 256), BF16),
            pltpu.VMEM((8, 16, 128), F32),
            pltpu.VMEM((8, 16, 128), F32),
            pltpu.VMEM((16, 128), F32),
            pltpu.VMEM((8, 16, 128), F32),
            pltpu.VMEM((128, 128), F32),
            pltpu.VMEM((4, 2, 256, 256), BF16),
            pltpu.VMEM((4, 256, 256), BF16),
            pltpu.VMEM((4, 256, 256), BF16),
            pltpu.VMEM((4, 256, 256), BF16),
            pltpu.VMEM((2, 128, 256), BF16),
            pltpu.VMEM((128, 256), BF16),
            pltpu.VMEM((128, 256), BF16),
            pltpu.VMEM((512, 768), BF16),
            pltpu.VMEM((384, 768), BF16),
            pltpu.VMEM((256, 256), F32),
            pltpu.VMEM((8, 64, 128), BF16),
            pltpu.SemaphoreType.DMA((TAPS,)),
            pltpu.SemaphoreType.DMA((N_COPIES,)),
            pltpu.SemaphoreType.DMA((N_COPIES,)),
        ],
        compiler_params=pltpu.CompilerParams(
            collective_id=0, has_side_effects=True, vmem_limit_bytes=56 * 1024 * 1024
        ),
        cost_estimate=pl.CostEstimate(flops=4_000_000_000, bytes_accessed=10_000_000, transcendentals=0),
    )(taps.reshape(4, 2048, 512), ln_gain, w_proj, conv_one, conv_two)
    return out.reshape(4, 2, 64, 4, 32).transpose(0, 1, 3, 2, 4).reshape(4, 8, 64, 32)


def solution(mesh):
    placed = (
        P(None, "dp", "mp", None, "section"),
        P(None, "section"),
        P(None, ("section", "dp", "mp"), None),
        P(("dp", "mp"), None),
        P(("dp", "mp"), "section"),
    )
    return jax.shard_map(
        per_device,
        mesh=mesh,
        in_specs=placed,
        out_specs=P("dp", "mp", None, "section"),
        check_vma=False,
    )
```

time: 420 us -> 73.8 us (0.18)
  the two profiles are of different devices: /device:TPU:8 before, /device:TPU:1 now
where the time goes in v1:
time: 73.8 us; the launch traced here: 73.6 us
  Pallas kernels  70.4 us (95%)
  local copies, waits for them, and re-layouts  3.13 us (4%)
    pallas_call x1, Pallas kernels, per_device(): pl.pallas_call(kernel, out_shape=jax.ShapeDtypeStruct((8, 64, 128), BF16)...  70.4 us
    pallas_call x1, local copies, waits for them, and re-layouts, per_device(): pl.pallas_call(kernel, out_shape=jax.ShapeDtypeStruct((8, 64, 128), BF16)...  1.75 us

profile of v1, /device:TPU:1, one launch (start us, length us, event | category | flops | bytes accessed | tf_op | source)
XLA Modules:
  0.0 73.6 jit_solution(12576124478586345163)
XLA Ops:
  0.0 1.4 %copy.8.c2_ref = bf16[72,32]{1,0:T(8,128)(2,1)} copy(bf16[72,32]{0,1:T(8,128)(2,1)} %param.9) | data formatting | bytes 9216 | tf_op args[4]
  1.4 70.4 %shard_map.55 = bf16[8,64,128]{2,1,0:T(8,128)(2,1)} custom-call(bf16[4,2048,512]{2,1,0:T(8,128)(2,1)} %bitcast.6, f32[4,512]{1,0:T(4,128)} %gain_ref.1, bf16[4,16,256]{2,1,0:T(8,128)(2,1)} %w_ref.1, bf16[72,256]{1,0:T(8,128)(2,1)} %c1_ref.1, bf16[72,32]{1,0:T(8,128)(2,1)} %copy.8.c2_ref), custom_call_target="tpu_custom_call" | custom-call | flops 4000000000 | bytes 10000000 | tf_op jit(solution)/shard_map/pallas_call | solution.py:339
  71.8 1.7 %copy.9 = bf16[8,64,128]{1,2,0:T(8,128)(2,1)} copy(bf16[8,64,128]{2,1,0:T(8,128)(2,1)} %shard_map.55) | data formatting | bytes 262144 | tf_op jit(solution)/shard_map/pallas_call | solution.py:339

commit v2 on v1

v2 whole, which is shorter than its diff:
```python
import jax
import jax.numpy as jnp
from jax import lax
from jax.experimental import pallas as pl
from jax.experimental.pallas import tpu as pltpu
from jax.sharding import PartitionSpec as P

D = 4096
TAPS = 4
MESH = pl.DeviceIdType.MESH
F32 = jnp.float32
BF16 = jnp.bfloat16
N_COPIES = 80


class Links:
    def __init__(self, send_sems, recv_sems):
        self.send_sems, self.recv_sems = send_sems, recv_sems
        self.used = 0
        self.copies = []

    def make(self, src, dst, to, recv_sem=None):
        copy = pltpu.make_async_remote_copy(
            src_ref=src,
            dst_ref=dst,
            send_sem=self.send_sems.at[self.used],
            recv_sem=self.recv_sems.at[self.used] if recv_sem is None else recv_sem,
            device_id=to,
            device_id_type=MESH,
        )
        self.used += 1
        return copy

    def start(self, src, dst, to, recv_sem=None):
        copy = self.make(src, dst, to, recv_sem)
        copy.start()
        self.copies.append(copy)
        return copy

    def finish(self):
        for copy in self.copies:
            copy.wait_send()


def received(copies):
    for copy in copies:
        copy.wait_recv()


def kernel(
    taps_hbm, gain_ref, w_ref, c1_ref, c2_ref, out_ref,
    taps, part, wall, gw, gsum, gcol, c2sq, c2pad, c2all, call_, conv, tot, tparts, tall, tcols,
    joint, jsib, jsum, jrecv, act, hsib, hcross, x1, x2, res, packed, arrived,
    tap_sems, send_sems, recv_sems, line_sems,
):
    sec, x, mp = lax.axis_index("section"), lax.axis_index("dp"), lax.axis_index("mp")
    zlo, core = sec // 2, sec % 2
    zhi, y = mp // 4, mp % 4
    links = Links(send_sems, recv_sems)

    reads = [pltpu.make_async_copy(taps_hbm.at[t], taps.at[t], tap_sems.at[t]) for t in range(TAPS)]
    for read in reads:
        read.start()

    peers = [{"section": (sec + k) % 8} for k in range(1, 8)]
    xs = [{"dp": (x + k) % 4} for k in (1, 3, 2)]
    ys = [{"mp": zhi * 4 + (y + k) % 4} for k in (1, 3, 2)]
    z_far = {"mp": (1 - zhi) * 4 + y}
    sibling = {"section": zlo * 2 + 1 - core}
    has_cross = jnp.where(core == 0, mp > 0, mp < 7)
    cross = {"mp": (mp + 7 + 2 * core) % 8, "section": zlo * 2 + 1 - core}

    hcross[...] = jnp.zeros_like(hcross)
    jrecv[...] = jnp.zeros_like(jrecv)

    barrier = pltpu.get_barrier_semaphore()
    greeted = peers + xs + ys + [z_far]
    for device in greeted:
        pl.semaphore_signal(barrier, inc=1, device_id=device, device_id_type=MESH)

    @pl.when(has_cross)
    def _():
        pl.semaphore_signal(barrier, inc=1, device_id=cross, device_id_type=MESH)

    for t in range(TAPS):
        wall[t, x, zhi, y] = w_ref[t]
    c2sq[...] = jnp.zeros_like(c2sq)
    c2sq[0:32, 0:72] = c2_ref[...].astype(F32)
    rows = c2sq[...].T
    c2pad[...] = jnp.concatenate(
        [rows[0:24] + pltpu.roll(rows[24:48], 32, 1) + pltpu.roll(rows[48:72], 64, 1), jnp.zeros((8, 128), F32)], axis=0
    ).astype(BF16)
    gcol[...] = jnp.zeros_like(gcol)
    gcol[0:4, :] = gain_ref[...]
    pl.semaphore_wait(barrier, len(greeted) + has_cross.astype(jnp.int32))

    every = slice(None)

    def w_view(half, xi, yi, zi):
        return wall.at[2 * half : 2 * half + 2, xi, zi, yi]

    def c_view(half, xi, yi, zi):
        return call_.at[core, xi, zi, yi, (slice(0, 48), slice(48, 80))[half]]

    def first(view, zi):
        got = []
        for half, to in ((0, xs), (1, ys)):
            s = view(half, x, y, zi)
            got.append([links.start(s, s, device) for device in to])
        return got

    def second(view, zi, got):
        sent = []
        received(got[0])
        s = view(0, every, y, zi)
        sent += [links.start(s, s, device) for device in ys]
        received(got[1])
        s = view(1, x, every, zi)
        sent += [links.start(s, s, device) for device in xs]
        return sent

    mine = wall.at[:, x, zhi, y]
    w_far = links.start(mine, mine, z_far)
    w_near1 = first(w_view, zhi)

    lane = lax.broadcasted_iota(jnp.int32, (128, 128), 1)

    def stats(t, total):
        def body(b, total):
            v = taps[t, pl.ds(pl.multiple_of(b * 128, 128), 128), :].astype(F32)
            s = jnp.sum(v, axis=1, keepdims=True)
            q = jnp.sum(v * v, axis=1, keepdims=True)
            total = jnp.where(lane == b * 8 + t, s, total)
            return jnp.where(lane == b * 8 + 4 + t, q, total)

        return lax.fori_loop(0, 16, body, total)

    reads[0].wait()
    total = stats(0, jnp.zeros((128, 128), F32))
    reads[1].wait()
    total = stats(1, total)
    w_near2 = second(w_view, zhi, w_near1)
    w_far.wait_recv()
    w_far1 = first(w_view, 1 - zhi)
    reads[2].wait()
    total = stats(2, total)
    reads[3].wait()
    total = stats(3, total)
    tot[...] = total.T.reshape(8, 16, 128)
    sent = [links.start(tot.at[(sec + k) % 8], tparts.at[k], peers[k - 1]) for k in range(1, 8)]
    w_far2 = second(w_view, 1 - zhi, w_far1)
    c2_got = [links.start(c2pad, c2all.at[k], peers[k - 1]) for k in range(1, 8)]

    received(sent)
    own = tot[sec]
    for k in range(1, 8):
        own = own + tparts[k]
    outs = []
    for blk in range(2):
        mean = own[8 * blk : 8 * blk + 4] / D
        var = jnp.maximum(own[8 * blk + 4 : 8 * blk + 8] / D - mean * mean, 0.0)
        r = lax.rsqrt(var + 1e-6)
        outs += [r, r * mean]
    tall[sec] = jnp.concatenate(outs, axis=0)
    mine = tall.at[sec]
    sent = [links.start(mine, mine, peers[k - 1]) for k in range(1, 8)]

    received(c2_got)
    c2all[0] = c2pad[...]
    lanes24 = lax.broadcasted_iota(jnp.int32, (24, 128), 1) // 32
    sides = [[jnp.zeros((24, 128), F32) for _ in range(3)] for _ in range(2)]
    for d in range(8):
        block = c2all[(sec - d + 8) % 8].astype(F32)[0:24]
        for g in range(3):
            turn = (32 * (d % 4 - g)) % 128
            moved = pltpu.roll(block, turn, 1) if turn else block
            sides[d // 4][g] = jnp.where(lanes24 == d % 4, moved, sides[d // 4][g])
    blank = jnp.zeros((8, 256), F32)
    one = jnp.concatenate([c1_ref[...].astype(F32), blank], axis=0)
    two = jnp.concatenate([jnp.concatenate(side, axis=0) for side in sides], axis=1)
    two = jnp.concatenate([two, blank], axis=0)
    call_[core, x, zhi, y] = jnp.where(core == 0, one, two).astype(BF16)
    mine = call_.at[core, x, zhi, y]
    c_far = links.start(mine, mine, z_far)

    gains = gcol[...].T
    received(w_near2)
    received(w_far2)

    def project(t):
        scaled = (wall[t].reshape(512, 256).astype(F32) * gains[:, t : t + 1]).astype(BF16)
        gw[t] = scaled
        gsum[t] = jnp.sum(scaled.astype(F32), axis=0, keepdims=True)

        def body(i, _):
            rows = pl.ds(pl.multiple_of(i * 512, 512), 512)
            part[t, rows, :] = jnp.dot(taps[t, rows, :], gw[t], preferred_element_type=F32)
            return 0

        lax.fori_loop(0, 4, body, 0)

    project(0)
    project(1)
    c_far.wait_recv()
    c_got = first(c_view, every)
    project(2)
    project(3)

    received(sent)
    tcols[...] = tall[...].reshape(128, 128).T

    def combine(b):
        cols = pltpu.roll(tcols[...], (128 - 8 * b) % 128, 1)
        rows = pl.ds(pl.multiple_of(b * 128, 128), 128)
        acc = cols[:, 0:1] * part[0, rows, :] - cols[:, 4:5] * gsum[0]
        for t in range(1, TAPS):
            acc = acc + (cols[:, t : t + 1] * part[t, rows, :] - cols[:, 4 + t : 5 + t] * gsum[t])
        return acc.astype(BF16)

    def strips(image):
        def strip(h, _):
            half = lax.rem(h + 1 - core + 2, 2)
            for blk in range(2):
                joint[image, half, blk * 128 : blk * 128 + 128] = combine(image * 4 + half * 2 + blk)
            return 0

        lax.fori_loop(0, 2, strip, 0)

    place = jnp.where(zlo < 2, zlo, 3 - zlo)
    end = place == 0

    def absolute(p):
        return jnp.where(zlo < 2, p, 3 - p)

    images = [absolute(jnp.where(end, a, b)) for a, b in ((3, 2), (2, 0), (1, 3))] + [zlo]
    chips = [absolute(jnp.where(end, a, b)) for a, b in ((1, 2), (2, 0), (1, 3))]
    slots = [jnp.where(end, 4, zlo), zlo, zlo]

    def line_copy(k):
        return links.start(
            jsum.at[k], jrecv.at[slots[k]], {"section": chips[k] * 2 + core}, line_sems.at[slots[k]]
        )

    def line_arrived(slot):
        pltpu.make_async_remote_copy(
            src_ref=jsum.at[0], dst_ref=jrecv.at[slot], send_sem=send_sems.at[0], recv_sem=line_sems.at[slot],
            device_id=sibling, device_id_type=MESH,
        ).wait_recv()

    swaps = {}

    def onward(k):
        swaps[k].wait_recv()
        value = joint[images[k], core].astype(F32) + jsib[k].astype(F32)
        if k == 2:
            @pl.when(jnp.logical_not(end))
            def _():
                line_arrived(4)

            value = value + jrecv[4].astype(F32)
        jsum[k] = value.astype(BF16)
        line_copy(k)

    for k in range(4):
        strips(images[k])
        swaps[k] = links.start(joint.at[images[k], 1 - core], jsib.at[k], sibling)
        if k == 2:
            c_got = second(c_view, every, c_got)
        if k in (1, 2):
            onward(k - 1)
    onward(2)
    swaps[3].wait_recv()
    own = joint[zlo, core].astype(F32) + jsib[3].astype(F32)
    for s in range(4):
        far_end = 3 if s == 0 else 0 if s == 3 else -1

        @pl.when(jnp.logical_and(zlo != s, zlo != far_end))
        def _(s=s):
            line_arrived(s)

    for s in range(4):
        own = own + jrecv[s].astype(F32)
    res[...] = own
    act[...] = jnp.maximum(own, 0.0).astype(BF16).reshape(2, 128, 256)
    h1 = links.start(act.at[1 - core], hsib, sibling)
    h2 = links.make(act.at[core], hcross, cross)

    @pl.when(has_cross)
    def _():
        h2.start()

    received(c_got)
    whole = call_.at[core]
    c_swap = links.start(whole, whole, sibling)

    def unpack(which):
        def body(p, _):
            i, j, l = p // 4, (p // 2) % 2, 2 * (p % 2)
            one = call_[which, i, j, l].astype(F32)[0:72]
            two = call_[which, i, j, l + 1].astype(F32)[0:72]
            conv[which, pl.ds(pl.multiple_of(p * 144, 16), 144), :] = jnp.concatenate([one, two], axis=0).astype(BF16)
            return 0

        lax.fori_loop(0, 16, body, 0)

    unpack(core)
    c_swap.wait_recv()
    unpack(1 - core)
    h1.wait_recv()

    @pl.when(has_cross)
    def _():
        h2.wait_recv()
        h2.wait_send()

    def columns(value, x_ref, rows):
        col = lax.broadcasted_iota(jnp.int32, (rows, 256), 0) % 64
        x_ref[:, 0:256] = jnp.where(col == 0, 0.0, pltpu.roll(value, 1, 0)).astype(BF16)
        x_ref[:, 256:512] = value.astype(BF16)
        x_ref[:, 512:768] = jnp.where(col == 63, 0.0, pltpu.roll(value, rows - 1, 0)).astype(BF16)

    near, far = hsib[...].astype(F32), hcross[...].astype(F32)
    above = jnp.where(core == 0, far, near)
    below = jnp.where(core == 0, near, far)
    columns(jnp.concatenate([above, jnp.maximum(res[...], 0.0), below], axis=0), x1, 512)

    mid = jnp.dot(x1[0:384], conv[0, 0:768], preferred_element_type=F32)
    mid = mid + jnp.dot(x1[64:448], conv[0, 768:1536], preferred_element_type=F32)
    mid = mid + jnp.dot(x1[128:512], conv[0, 1536:2304], preferred_element_type=F32)
    row = lax.broadcasted_iota(jnp.int32, (384, 256), 0)
    top = jnp.logical_and(mp == 0, core == 0)
    bottom = jnp.logical_and(mp == 7, core == 1)
    outside = jnp.logical_or(jnp.logical_and(top, row < 64), jnp.logical_and(bottom, row >= 320))
    columns(jnp.where(outside, 0.0, jnp.maximum(mid, 0.0)), x2, 384)
    fin = res[...] + jnp.dot(x2[0:256], conv[1, 0:768], preferred_element_type=F32)
    fin = fin + jnp.dot(x2[64:320], conv[1, 768:1536], preferred_element_type=F32)
    fin = fin + jnp.dot(x2[128:384], conv[1, 1536:2304], preferred_element_type=F32)

    group = lax.broadcasted_iota(jnp.int32, (64, 128), 1) // 32
    for d in range(8):
        got = jnp.zeros((64, 128), F32)
        for g in range(4):
            block = fin[64 * g : 64 * g + 64, 128 * (d // 4) : 128 * (d // 4) + 128]
            turn = (32 * (g - d % 4)) % 128
            block = pltpu.roll(block, turn, 1) if turn else block
            got = jnp.where(group == g, block, got)
        packed[d] = got.astype(BF16)
    outs = [links.start(packed.at[(sec + k) % 8], arrived.at[k], peers[k - 1]) for k in range(1, 8)]
    arrived[0] = packed[sec]
    for k in range(8):
        if k:
            outs[k - 1].wait_recv()
        out_ref[(sec - k + 8) % 8] = arrived[k].astype(F32).T.astype(BF16)
    links.finish()


def per_device(taps, ln_gain, w_proj, conv_one, conv_two):
    vmem = pl.BlockSpec(memory_space=pltpu.VMEM)
    out = pl.pallas_call(
        kernel,
        out_shape=jax.ShapeDtypeStruct((8, 128, 64), BF16),
        in_specs=[pl.BlockSpec(memory_space=pl.ANY)] + [vmem] * 4,
        out_specs=vmem,
        scratch_shapes=[
            pltpu.VMEM((4, 2048, 512), BF16),
            pltpu.VMEM((4, 2048, 256), F32),
            pltpu.VMEM((4, 4, 2, 4, 16, 256), BF16),
            pltpu.VMEM((4, 512, 256), BF16),
            pltpu.VMEM((4, 1, 256), F32),
            pltpu.VMEM((128, 512), F32),
            pltpu.VMEM((128, 128), F32),
            pltpu.VMEM((32, 128), BF16),
            pltpu.VMEM((8, 32, 128), BF16),
            pltpu.VMEM((2, 4, 2, 4, 80, 256), BF16),
            pltpu.VMEM((2, 2304, 256), BF16),
            pltpu.VMEM((8, 16, 128), F32),
            pltpu.VMEM((8, 16, 128), F32),
            pltpu.VMEM((8, 16, 128), F32),
            pltpu.VMEM((128, 128), F32),
            pltpu.VMEM((4, 2, 256, 256), BF16),
            pltpu.VMEM((4, 256, 256), BF16),
            pltpu.VMEM((3, 256, 256), BF16),
            pltpu.VMEM((5, 256, 256), BF16),
            pltpu.VMEM((2, 128, 256), BF16),
            pltpu.VMEM((128, 256), BF16),
            pltpu.VMEM((128, 256), BF16),
            pltpu.VMEM((512, 768), BF16),
            pltpu.VMEM((384, 768), BF16),
            pltpu.VMEM((256, 256), F32),
            pltpu.VMEM((8, 64, 128), BF16),
            pltpu.VMEM((8, 64, 128), BF16),
            pltpu.SemaphoreType.DMA((TAPS,)),
            pltpu.SemaphoreType.DMA((N_COPIES,)),
            pltpu.SemaphoreType.DMA((N_COPIES,)),
            pltpu.SemaphoreType.DMA((5,)),
        ],
        compiler_params=pltpu.CompilerParams(
            collective_id=0, has_side_effects=True, vmem_limit_bytes=56 * 1024 * 1024
        ),
        cost_estimate=pl.CostEstimate(flops=4_000_000_000, bytes_accessed=10_000_000, transcendentals=0),
    )(taps.reshape(4, 2048, 512), ln_gain, w_proj, conv_one, conv_two.T)
    return out.reshape(4, 8, 32, 64).transpose(0, 1, 3, 2)


def solution(mesh):
    placed = (
        P(None, "dp", "mp", None, "section"),
        P(None, "section"),
        P(None, ("section", "dp", "mp"), None),
        P(("dp", "mp"), None),
        P(("dp", "mp"), "section"),
    )
    return jax.shard_map(
        per_device,
        mesh=mesh,
        in_specs=placed,
        out_specs=P("dp", "mp", None, "section"),
        check_vma=False,
    )
```

time: 73.8 us -> 61.5 us (0.83)
  Pallas kernels: 70.4 us -> 59.7 us
  local copies, waits for them, and re-layouts: 3.13 us -> 1.67 us
    pallas_call x1, Pallas kernels: 70.4 us -> 59.7 us  [per_device(): pl.pallas_call(kernel, out_shape=jax.ShapeDtypeStruct((8, 128, 64), BF16)...]
    pallas_call x1 -> x0, local copies, waits for them, and re-layouts: 1.75 us -> none  [per_device(): pl.pallas_call(kernel, out_shape=jax.ShapeDtypeStruct((8, 64, 128), BF16)...]
where the time goes in v2:
time: 61.5 us; the launch traced here: 61.3 us
  Pallas kernels  59.7 us (97%)
  local copies, waits for them, and re-layouts  1.67 us (3%)
    pallas_call x1, Pallas kernels, per_device(): pl.pallas_call(kernel, out_shape=jax.ShapeDtypeStruct((8, 128, 64), BF16)...  59.7 us
    unnamed x1, local copies, waits for them, and re-layouts  1.67 us

profile of v2, /device:TPU:1, one launch (start us, length us, event | category | flops | bytes accessed | tf_op | source)
XLA Modules:
  0.0 61.3 jit_solution(4343621913686107668)
XLA Ops:
  0.0 59.7 %shard_map.55 = bf16[8,128,64]{2,1,0:T(8,128)(2,1)} custom-call(bf16[4,2048,512]{2,1,0:T(8,128)(2,1)} %bitcast.6, f32[4,512]{1,0:T(4,128)} %gain_ref.1, bf16[4,16,256]{2,1,0:T(8,128)(2,1)} %w_ref.1, bf16[72,256]{1,0:T(8,128)(2,1)} %c1_ref.1, bf16[32,72]{1,0:T(8,128)(2,1)} %bitcast.7), custom_call_target="tpu_custom_call" | custom-call | flops 4000000000 | bytes 10000000 | tf_op jit(solution)/shard_map/pallas_call | solution.py:359
  59.7 1.7 %copy.7 = bf16[4,8,64,32]{2,3,1,0:T(8,128)(2,1)} copy(bf16[4,8,64,32]{2,3,1,0:T(8,128)(2,1)} %bitcast.5) | data formatting | bytes 262144

commit v3 on v2

v3 whole, which is shorter than its diff:
```python
import jax
import jax.numpy as jnp
from jax import lax
from jax.experimental import pallas as pl
from jax.experimental.pallas import tpu as pltpu
from jax.sharding import PartitionSpec as P

D = 4096
TAPS = 4
MESH = pl.DeviceIdType.MESH
F32 = jnp.float32
BF16 = jnp.bfloat16
N_COPIES = 112


class Links:
    def __init__(self, send_sems, recv_sems):
        self.send_sems, self.recv_sems = send_sems, recv_sems
        self.used = 0
        self.copies = []

    def make(self, src, dst, to, recv_sem=None):
        copy = pltpu.make_async_remote_copy(
            src_ref=src,
            dst_ref=dst,
            send_sem=self.send_sems.at[self.used],
            recv_sem=self.recv_sems.at[self.used] if recv_sem is None else recv_sem,
            device_id=to,
            device_id_type=MESH,
        )
        self.used += 1
        return copy

    def start(self, src, dst, to, recv_sem=None):
        copy = self.make(src, dst, to, recv_sem)
        copy.start()
        self.copies.append(copy)
        return copy

    def finish(self):
        for copy in self.copies:
            copy.wait_send()


def received(copies):
    for copy in copies:
        copy.wait_recv()


def kernel(
    taps_hbm, gain_ref, w_ref, c1_ref, c2_ref, out_ref,
    taps, part, wall, gw, gsum, gcol, c2sq, c2pad, c2all, call_, conv, tot, tparts, tall, tcols,
    joint, jsib, jsum, jrecv, act, hsib, hcross, x1, x2, res, packed, arrived,
    tap_sems, send_sems, recv_sems, line_sems,
):
    sec, x, mp = lax.axis_index("section"), lax.axis_index("dp"), lax.axis_index("mp")
    zlo, core = sec // 2, sec % 2
    zhi, y = mp // 4, mp % 4
    links = Links(send_sems, recv_sems)

    reads = [pltpu.make_async_copy(taps_hbm.at[t], taps.at[t], tap_sems.at[t]) for t in range(TAPS)]
    for read in reads:
        read.start()

    peers = [{"section": (sec + k) % 8} for k in range(1, 8)]
    xs = [{"dp": (x + k) % 4} for k in (1, 3, 2)]
    ys = [{"mp": zhi * 4 + (y + k) % 4} for k in (1, 3, 2)]
    plane = [
        {"dp": (x + i) % 4, "mp": zhi * 4 + (y + j) % 4} for i in range(4) for j in range(4) if i or j
    ]
    z_far = {"mp": (1 - zhi) * 4 + y}
    sibling = {"section": zlo * 2 + 1 - core}
    has_cross = jnp.where(core == 0, mp > 0, mp < 7)
    cross = {"mp": (mp + 7 + 2 * core) % 8, "section": zlo * 2 + 1 - core}

    hcross[...] = jnp.zeros_like(hcross)
    jrecv[...] = jnp.zeros_like(jrecv)

    barrier = pltpu.get_barrier_semaphore()
    greeted = peers + plane + [z_far]
    for device in greeted:
        pl.semaphore_signal(barrier, inc=1, device_id=device, device_id_type=MESH)

    @pl.when(has_cross)
    def _():
        pl.semaphore_signal(barrier, inc=1, device_id=cross, device_id_type=MESH)

    for t in range(TAPS):
        wall[t, x, zhi, y] = w_ref[t]
    pl.semaphore_wait(barrier, len(greeted) + has_cross.astype(jnp.int32))

    every = slice(None)

    def c_view(half, xi, yi, zi):
        return call_.at[core, xi, zi, yi, (slice(0, 48), slice(48, 80))[half]]

    def first(view, zi):
        got = []
        for half, to in ((0, xs), (1, ys)):
            s = view(half, x, y, zi)
            got.append([links.start(s, s, device) for device in to])
        return got

    def second(view, zi, got):
        sent = []
        received(got[0])
        s = view(0, every, y, zi)
        sent += [links.start(s, s, device) for device in ys]
        received(got[1])
        s = view(1, x, every, zi)
        sent += [links.start(s, s, device) for device in xs]
        return sent

    mine = wall.at[:, x, zhi, y]
    w_far = links.start(mine, mine, z_far)
    w_got = [links.start(mine, mine, device) for device in plane]

    lane = lax.broadcasted_iota(jnp.int32, (128, 128), 1)

    def stats(t, total):
        reads[t].wait()
        v = taps[t].astype(F32)
        s = jnp.sum(v, axis=1, keepdims=True)
        q = jnp.sum(v * v, axis=1, keepdims=True)
        for b in range(16):
            total = jnp.where(lane == b * 8 + t, s[128 * b : 128 * b + 128], total)
            total = jnp.where(lane == b * 8 + 4 + t, q[128 * b : 128 * b + 128], total)
        return total

    c2sq[...] = jnp.zeros_like(c2sq)
    c2sq[0:32, 0:72] = c2_ref[...].astype(F32)
    rows = c2sq[...].T
    c2pad[...] = jnp.concatenate(
        [rows[0:24] + pltpu.roll(rows[24:48], 32, 1) + pltpu.roll(rows[48:72], 64, 1), jnp.zeros((8, 128), F32)], axis=0
    ).astype(BF16)
    gcol[...] = jnp.zeros_like(gcol)
    gcol[0:4, :] = gain_ref[...]
    c2_got = [links.start(c2pad, c2all.at[k], peers[k - 1]) for k in range(1, 8)]

    total = jnp.zeros((128, 128), F32)
    for t in range(TAPS):
        total = stats(t, total)
    tot[...] = total.T.reshape(8, 16, 128)
    sent = [links.start(tot.at[(sec + k) % 8], tparts.at[k], peers[k - 1]) for k in range(1, 8)]
    w_far.wait_recv()
    mine = wall.at[:, x, 1 - zhi, y]
    w_got += [links.start(mine, mine, device) for device in plane]

    received(c2_got)
    c2all[0] = c2pad[...]
    lanes24 = lax.broadcasted_iota(jnp.int32, (24, 128), 1) // 32
    sides = [[jnp.zeros((24, 128), F32) for _ in range(3)] for _ in range(2)]
    for d in range(8):
        block = c2all[(sec - d + 8) % 8].astype(F32)[0:24]
        for g in range(3):
            turn = (32 * (d % 4 - g)) % 128
            moved = pltpu.roll(block, turn, 1) if turn else block
            sides[d // 4][g] = jnp.where(lanes24 == d % 4, moved, sides[d // 4][g])
    blank = jnp.zeros((8, 256), F32)
    one = jnp.concatenate([c1_ref[...].astype(F32), blank], axis=0)
    two = jnp.concatenate([jnp.concatenate(side, axis=0) for side in sides], axis=1)
    two = jnp.concatenate([two, blank], axis=0)
    call_[core, x, zhi, y] = jnp.where(core == 0, one, two).astype(BF16)
    mine = call_.at[core, x, zhi, y]
    c_far = links.start(mine, mine, z_far)

    received(sent)
    own = tot[sec]
    for k in range(1, 8):
        own = own + tparts[k]
    outs = []
    for blk in range(2):
        mean = own[8 * blk : 8 * blk + 4] / D
        var = jnp.maximum(own[8 * blk + 4 : 8 * blk + 8] / D - mean * mean, 0.0)
        r = lax.rsqrt(var + 1e-6)
        outs += [r, r * mean]
    tall[sec] = jnp.concatenate(outs, axis=0)
    mine = tall.at[sec]
    sent = [links.start(mine, mine, peers[k - 1]) for k in range(1, 8)]

    gains = gcol[...].T
    c_far.wait_recv()
    c_got = first(c_view, every)
    received(w_got)

    for t in range(TAPS):
        scaled = (wall[t].reshape(512, 256).astype(F32) * gains[:, t : t + 1]).astype(BF16)
        gw[t] = scaled
        gsum[t] = jnp.sum(scaled.astype(F32), axis=0, keepdims=True)

    received(sent)
    tcols[...] = tall[...].reshape(128, 128).T

    def strip(image, half):
        rows = pl.ds(pl.multiple_of(image * 512 + half * 256, 256), 256)
        for t in range(TAPS):
            part[t] = jnp.dot(taps[t, rows, :], gw[t], preferred_element_type=F32)
        for blk in range(2):
            cols = pltpu.roll(tcols[...], (128 - 8 * (image * 4 + half * 2 + blk)) % 128, 1)
            span = slice(blk * 128, blk * 128 + 128)
            acc = cols[:, 0:1] * part[0, span, :] - cols[:, 4:5] * gsum[0]
            for t in range(1, TAPS):
                acc = acc + (cols[:, t : t + 1] * part[t, span, :] - cols[:, 4 + t : 5 + t] * gsum[t])
            joint[image, half, span] = acc.astype(BF16)

    place = jnp.where(zlo < 2, zlo, 3 - zlo)
    end = place == 0

    def absolute(p):
        return jnp.where(zlo < 2, p, 3 - p)

    images = [absolute(jnp.where(end, a, b)) for a, b in ((3, 2), (2, 0), (1, 3))] + [zlo]
    chips = [absolute(jnp.where(end, a, b)) for a, b in ((1, 2), (2, 0), (1, 3))]
    slots = [jnp.where(end, 4, zlo), zlo, zlo]

    def line_send(k, h):
        links.start(
            jsum.at[k, h], jrecv.at[slots[k], h], {"section": chips[k] * 2 + core}, line_sems.at[slots[k], h]
        )

    def line_arrived(slot, h):
        pltpu.make_async_remote_copy(
            src_ref=jsum.at[0, 0], dst_ref=jrecv.at[slot, h], send_sem=send_sems.at[0],
            recv_sem=line_sems.at[slot, h], device_id=sibling, device_id_type=MESH,
        ).wait_recv()

    swaps = {}

    def swap(k):
        strip(images[k], 1 - core)
        swaps[k] = links.start(joint.at[images[k], 1 - core], jsib.at[k], sibling)

    def pair(k, h):
        span = pl.ds(pl.multiple_of(128 * h, 128), 128)
        return joint[images[k], core, span].astype(F32) + jsib[k, span].astype(F32)

    def onward(k):
        swaps[k].wait_recv()
        for h in halves:
            value = pair(k, h)
            if k == 2:
                @pl.when(jnp.logical_not(end))
                def _(h=h):
                    line_arrived(4, h)

                value = value + jrecv[4, h].astype(F32)
            jsum[k, h] = value.astype(BF16)
            line_send(k, h)

    def joined(h):
        for s in range(4):
            far_end = 3 if s == 0 else 0 if s == 3 else -1

            @pl.when(jnp.logical_and(zlo != s, zlo != far_end))
            def _(s=s):
                line_arrived(s, h)

        value = pair(3, h)
        for s in range(4):
            value = value + jrecv[s, h].astype(F32)
        res[h] = value
        act[h] = jnp.maximum(value, 0.0).astype(BF16)

    def unpack(which):
        def body(i, _):
            for j in range(2):
                for l in (0, 2):
                    one = call_[which, i, j, l].astype(F32)[0:72]
                    two = call_[which, i, j, l + 1].astype(F32)[0:72]
                    at = pl.ds(pl.multiple_of(i * 576, 16) + 288 * j + 72 * l, 144)
                    conv[which, at, :] = jnp.concatenate([one, two], axis=0).astype(BF16)
            return 0

        lax.fori_loop(0, 4, body, 0)

    halves = (core, 1 - core)
    swap(0)
    swap(1)
    strip(images[0], core)
    onward(0)
    c_got = second(c_view, every, c_got)
    swap(2)
    strip(images[1], core)
    onward(1)
    swap(3)
    strip(images[2], core)
    strip(images[3], core)
    onward(2)
    received(c_got)
    whole = call_.at[core]
    c_swap = links.start(whole, whole, sibling)
    swaps[3].wait_recv()
    joined(core)
    h2 = links.make(act.at[core], hcross, cross)

    @pl.when(has_cross)
    def _():
        h2.start()

    unpack(core)
    joined(1 - core)
    h1 = links.start(act.at[1 - core], hsib, sibling)
    c_swap.wait_recv()
    unpack(1 - core)

    def columns(value, x_ref, start):
        rows = value.shape[0]
        span = pl.ds(pl.multiple_of(start, 64), rows)
        col = lax.broadcasted_iota(jnp.int32, (rows, 256), 0) % 64
        x_ref[span, 0:256] = jnp.where(col == 0, 0.0, pltpu.roll(value, 1, 0)).astype(BF16)
        x_ref[span, 256:512] = value.astype(BF16)
        x_ref[span, 512:768] = jnp.where(col == 63, 0.0, pltpu.roll(value, rows - 1, 0)).astype(BF16)

    def convolved(x_ref, which, start, rows):
        total = jnp.zeros((rows, 256), F32)
        for a in range(3):
            span = pl.ds(pl.multiple_of(start + 64 * a, 64), rows)
            total = total + jnp.dot(
                x_ref[span], conv[which, 768 * a : 768 * a + 768], preferred_element_type=F32
            )
        return total

    def finished(which_half, p):
        total = convolved(x2, 1, 128 * which_half, 128) + res[which_half]
        packed[p] = total.T.astype(BF16).reshape(8, 32, 128)
        return [links.start(packed.at[p, (sec + k) % 8], arrived.at[p, k], peers[k - 1]) for k in range(1, 8)]

    columns(jnp.maximum(res[...].reshape(256, 256), 0.0), x1, 128)
    h1.wait_recv()
    columns(hsib[...].astype(F32), x1, 384 * (1 - core))
    columns(jnp.maximum(convolved(x1, 0, 128 * (1 - core), 256), 0.0), x2, 128 * (1 - core))
    outs = [finished(1 - core, 0)]

    @pl.when(has_cross)
    def _():
        h2.wait_recv()
        h2.wait_send()

    columns(hcross[...].astype(F32), x1, 384 * core)
    row = lax.broadcasted_iota(jnp.int32, (128, 256), 0) // 64
    outside = jnp.logical_and(row == core, jnp.logical_not(has_cross))
    mid = jnp.where(outside, 0.0, jnp.maximum(convolved(x1, 0, 256 * core, 128), 0.0))
    columns(mid, x2, 256 * core)
    outs.append(finished(core, 1))

    for p in range(2):
        arrived[p, 0] = packed[p, sec]
        for k in range(8):
            if k:
                outs[p][k - 1].wait_recv()
            their = (core + k) % 2
            block = arrived[p, k].astype(F32)
            for r, rows in ((0, block), (1, pltpu.roll(block, 64, 1))):
                at = 64 * (1 - their if p == 0 else their) + 32 * r
                out_ref[(sec - k + 8) % 8, pl.ds(pl.multiple_of(at, 32), 32), :] = rows[:, 0:64].astype(BF16)
    links.finish()


def per_device(taps, ln_gain, w_proj, conv_one, conv_two):
    vmem = pl.BlockSpec(memory_space=pltpu.VMEM)
    out = pl.pallas_call(
        kernel,
        out_shape=jax.ShapeDtypeStruct((8, 128, 64), BF16),
        in_specs=[pl.BlockSpec(memory_space=pl.ANY)] + [vmem] * 4,
        out_specs=vmem,
        scratch_shapes=[
            pltpu.VMEM((4, 2048, 512), BF16),
            pltpu.VMEM((4, 256, 256), F32),
            pltpu.VMEM((4, 4, 2, 4, 16, 256), BF16),
            pltpu.VMEM((4, 512, 256), BF16),
            pltpu.VMEM((4, 1, 256), F32),
            pltpu.VMEM((128, 512), F32),
            pltpu.VMEM((128, 128), F32),
            pltpu.VMEM((32, 128), BF16),
            pltpu.VMEM((8, 32, 128), BF16),
            pltpu.VMEM((2, 4, 2, 4, 80, 256), BF16),
            pltpu.VMEM((2, 2304, 256), BF16),
            pltpu.VMEM((8, 16, 128), F32),
            pltpu.VMEM((8, 16, 128), F32),
            pltpu.VMEM((8, 16, 128), F32),
            pltpu.VMEM((128, 128), F32),
            pltpu.VMEM((4, 2, 256, 256), BF16),
            pltpu.VMEM((4, 256, 256), BF16),
            pltpu.VMEM((3, 2, 128, 256), BF16),
            pltpu.VMEM((5, 2, 128, 256), BF16),
            pltpu.VMEM((2, 128, 256), BF16),
            pltpu.VMEM((128, 256), BF16),
            pltpu.VMEM((128, 256), BF16),
            pltpu.VMEM((512, 768), BF16),
            pltpu.VMEM((384, 768), BF16),
            pltpu.VMEM((2, 128, 256), F32),
            pltpu.VMEM((2, 8, 32, 128), BF16),
            pltpu.VMEM((2, 8, 32, 128), BF16),
            pltpu.SemaphoreType.DMA((TAPS,)),
            pltpu.SemaphoreType.DMA((N_COPIES,)),
            pltpu.SemaphoreType.DMA((N_COPIES,)),
            pltpu.SemaphoreType.DMA((5, 2)),
        ],
        compiler_params=pltpu.CompilerParams(
            collective_id=0, has_side_effects=True, vmem_limit_bytes=56 * 1024 * 1024
        ),
        cost_estimate=pl.CostEstimate(flops=4_000_000_000, bytes_accessed=10_000_000, transcendentals=0),
    )(taps.reshape(4, 2048, 512), ln_gain, w_proj, conv_one, conv_two.T)
    return out.reshape(4, 8, 32, 64).transpose(0, 1, 3, 2)


def solution(mesh):
    placed = (
        P(None, "dp", "mp", None, "section"),
        P(None, "section"),
        P(None, ("section", "dp", "mp"), None),
        P(("dp", "mp"), None),
        P(("dp", "mp"), "section"),
    )
    return jax.shard_map(
        per_device,
        mesh=mesh,
        in_specs=placed,
        out_specs=P("dp", "mp", None, "section"),
        check_vma=False,
    )
```

time: 61.5 us -> 55.2 us (0.90)
  Pallas kernels: 59.7 us -> 53.3 us
    pallas_call x1, Pallas kernels: 59.7 us -> 53.3 us  [per_device(): pl.pallas_call(kernel, out_shape=jax.ShapeDtypeStruct((8, 128, 64), BF16)...]
where the time goes in v3:
time: 55.2 us; the launch traced here: 55 us
  Pallas kernels  53.3 us (97%)
  local copies, waits for them, and re-layouts  1.67 us (3%)
    pallas_call x1, Pallas kernels, per_device(): pl.pallas_call(kernel, out_shape=jax.ShapeDtypeStruct((8, 128, 64), BF16)...  53.3 us
    unnamed x1, local copies, waits for them, and re-layouts  1.67 us

profile of v3, /device:TPU:1, one launch (start us, length us, event | category | flops | bytes accessed | tf_op | source)
XLA Modules:
  0.0 55.0 jit_solution(5394413442115510557)
XLA Ops:
  0.0 53.3 %shard_map.55 = bf16[8,128,64]{2,1,0:T(8,128)(2,1)} custom-call(bf16[4,2048,512]{2,1,0:T(8,128)(2,1)} %bitcast.6, f32[4,512]{1,0:T(4,128)} %gain_ref.1, bf16[4,16,256]{2,1,0:T(8,128)(2,1)} %w_ref.1, bf16[72,256]{1,0:T(8,128)(2,1)} %c1_ref.1, bf16[32,72]{1,0:T(8,128)(2,1)} %bitcast.7), custom_call_target="tpu_custom_call" | custom-call | flops 4000000000 | bytes 10000000 | tf_op jit(solution)/shard_map/pallas_call | solution.py:361
  53.3 1.7 %copy.7 = bf16[4,8,64,32]{2,3,1,0:T(8,128)(2,1)} copy(bf16[4,8,64,32]{2,3,1,0:T(8,128)(2,1)} %bitcast.5) | data formatting | bytes 262144

commit v4 on v3

--- a/solution.py
+++ b/solution.py
@@ -37,6 +37,10 @@
         self.copies.append(copy)
         return copy
 
+    def sent(self, copy):
+        copy.wait_send()
+        self.copies = [c for c in self.copies if c is not copy]
+
     def finish(self):
         for copy in self.copies:
             copy.wait_send()
@@ -49,9 +53,9 @@
 
 def kernel(
     taps_hbm, gain_ref, w_ref, c1_ref, c2_ref, out_ref,
-    taps, part, wall, gw, gsum, gcol, c2sq, c2pad, c2all, call_, conv, tot, tparts, tall, tcols,
+    taps, part, wall, gw, gsum, gcol, gains, c2sq, c2pad, c2all, call_, conv, tot, tparts, tall, tcols,
     joint, jsib, jsum, jrecv, act, hsib, hcross, x1, x2, res, packed, arrived,
-    tap_sems, send_sems, recv_sems, line_sems,
+    tap_sems, send_sems, recv_sems,
 ):
     sec, x, mp = lax.axis_index("section"), lax.axis_index("dp"), lax.axis_index("mp")
     zlo, core = sec // 2, sec % 2
@@ -65,19 +69,15 @@
     peers = [{"section": (sec + k) % 8} for k in range(1, 8)]
     xs = [{"dp": (x + k) % 4} for k in (1, 3, 2)]
     ys = [{"mp": zhi * 4 + (y + k) % 4} for k in (1, 3, 2)]
-    plane = [
-        {"dp": (x + i) % 4, "mp": zhi * 4 + (y + j) % 4} for i in range(4) for j in range(4) if i or j
-    ]
     z_far = {"mp": (1 - zhi) * 4 + y}
     sibling = {"section": zlo * 2 + 1 - core}
     has_cross = jnp.where(core == 0, mp > 0, mp < 7)
     cross = {"mp": (mp + 7 + 2 * core) % 8, "section": zlo * 2 + 1 - core}
 
     hcross[...] = jnp.zeros_like(hcross)
-    jrecv[...] = jnp.zeros_like(jrecv)
 
     barrier = pltpu.get_barrier_semaphore()
-    greeted = peers + plane + [z_far]
+    greeted = peers + xs + ys + [z_far]
     for device in greeted:
         pl.semaphore_signal(barrier, inc=1, device_id=device, device_id_type=MESH)
 
@@ -90,6 +90,9 @@
     pl.semaphore_wait(barrier, len(greeted) + has_cross.astype(jnp.int32))
 
     every = slice(None)
+
+    def w_view(half, xi, yi, zi):
+        return wall.at[2 * half : 2 * half + 2, xi, zi, yi]
 
     def c_view(half, xi, yi, zi):
         return call_.at[core, xi, zi, yi, (slice(0, 48), slice(48, 80))[half]]
@@ -113,7 +116,7 @@
 
     mine = wall.at[:, x, zhi, y]
     w_far = links.start(mine, mine, z_far)
-    w_got = [links.start(mine, mine, device) for device in plane]
+    w_near = first(w_view, zhi)
 
     lane = lax.broadcasted_iota(jnp.int32, (128, 128), 1)
 
@@ -137,14 +140,16 @@
     gcol[0:4, :] = gain_ref[...]
     c2_got = [links.start(c2pad, c2all.at[k], peers[k - 1]) for k in range(1, 8)]
 
+    gains[...] = gcol[...].T
     total = jnp.zeros((128, 128), F32)
-    for t in range(TAPS):
+    for t in range(3):
         total = stats(t, total)
+    w_far.wait_recv()
+    w_far = first(w_view, 1 - zhi)
+    w_near = second(w_view, zhi, w_near)
+    total = stats(3, total)
     tot[...] = total.T.reshape(8, 16, 128)
     sent = [links.start(tot.at[(sec + k) % 8], tparts.at[k], peers[k - 1]) for k in range(1, 8)]
-    w_far.wait_recv()
-    mine = wall.at[:, x, 1 - zhi, y]
-    w_got += [links.start(mine, mine, device) for device in plane]
 
     received(c2_got)
     c2all[0] = c2pad[...]
@@ -163,6 +168,7 @@
     call_[core, x, zhi, y] = jnp.where(core == 0, one, two).astype(BF16)
     mine = call_.at[core, x, zhi, y]
     c_far = links.start(mine, mine, z_far)
+    w_far = second(w_view, 1 - zhi, w_far)
 
     received(sent)
     own = tot[sec]
@@ -178,16 +184,24 @@
     mine = tall.at[sec]
     sent = [links.start(mine, mine, peers[k - 1]) for k in range(1, 8)]
 
-    gains = gcol[...].T
+    def scale(zi):
+        for t in range(TAPS):
+            sums = jnp.zeros((1, 256), F32)
+            for i in range(4):
+                rows = pl.ds(pl.multiple_of(i * 128 + zi * 64, 64), 64)
+                piece = wall[t, i, zi].reshape(64, 256).astype(F32) * gains[rows, t : t + 1]
+                piece = piece.astype(BF16)
+                gw[t, rows, :] = piece
+                sums = sums + jnp.sum(piece.astype(F32), axis=0, keepdims=True)
+            gsum[t] = gsum[t] + sums
+
+    gsum[...] = jnp.zeros_like(gsum)
+    received(w_near)
+    scale(zhi)
     c_far.wait_recv()
     c_got = first(c_view, every)
-    received(w_got)
-
-    for t in range(TAPS):
-        scaled = (wall[t].reshape(512, 256).astype(F32) * gains[:, t : t + 1]).astype(BF16)
-        gw[t] = scaled
-        gsum[t] = jnp.sum(scaled.astype(F32), axis=0, keepdims=True)
-
+    received(w_far)
+    scale(1 - zhi)
     received(sent)
     tcols[...] = tall[...].reshape(128, 128).T
 
@@ -203,27 +217,8 @@
                 acc = acc + (cols[:, t : t + 1] * part[t, span, :] - cols[:, 4 + t : 5 + t] * gsum[t])
             joint[image, half, span] = acc.astype(BF16)
 
-    place = jnp.where(zlo < 2, zlo, 3 - zlo)
-    end = place == 0
-
-    def absolute(p):
-        return jnp.where(zlo < 2, p, 3 - p)
-
-    images = [absolute(jnp.where(end, a, b)) for a, b in ((3, 2), (2, 0), (1, 3))] + [zlo]
-    chips = [absolute(jnp.where(end, a, b)) for a, b in ((1, 2), (2, 0), (1, 3))]
-    slots = [jnp.where(end, 4, zlo), zlo, zlo]
-
-    def line_send(k, h):
-        links.start(
-            jsum.at[k, h], jrecv.at[slots[k], h], {"section": chips[k] * 2 + core}, line_sems.at[slots[k], h]
-        )
-
-    def line_arrived(slot, h):
-        pltpu.make_async_remote_copy(
-            src_ref=jsum.at[0, 0], dst_ref=jrecv.at[slot, h], send_sem=send_sems.at[0],
-            recv_sem=line_sems.at[slot, h], device_id=sibling, device_id_type=MESH,
-        ).wait_recv()
-
+    images = [(zlo + k) % 4 for k in range(4)]
+    z_sent = {}
     swaps = {}
 
     def swap(k):
@@ -234,30 +229,17 @@
         span = pl.ds(pl.multiple_of(128 * h, 128), 128)
         return joint[images[k], core, span].astype(F32) + jsib[k, span].astype(F32)
 
-    def onward(k):
-        swaps[k].wait_recv()
-        for h in halves:
-            value = pair(k, h)
-            if k == 2:
-                @pl.when(jnp.logical_not(end))
-                def _(h=h):
-                    line_arrived(4, h)
-
-                value = value + jrecv[4, h].astype(F32)
-            jsum[k, h] = value.astype(BF16)
-            line_send(k, h)
-
-    def joined(h):
-        for s in range(4):
-            far_end = 3 if s == 0 else 0 if s == 3 else -1
-
-            @pl.when(jnp.logical_and(zlo != s, zlo != far_end))
-            def _(s=s):
-                line_arrived(s, h)
-
-        value = pair(3, h)
-        for s in range(4):
-            value = value + jrecv[s, h].astype(F32)
+    def onward(k, i):
+        h = halves[i]
+        jsum[k, h] = pair(k, h).astype(BF16)
+        z_sent[k, i] = links.start(jsum.at[k, h], jrecv.at[k, h], {"section": (sec + 2 * k) % 8})
+
+    def joined(i):
+        h = halves[i]
+        value = pair(0, h)
+        for k in range(1, 4):
+            z_sent[k, i].wait_recv()
+            value = value + jrecv[k, h].astype(F32)
         res[h] = value
         act[h] = jnp.maximum(value, 0.0).astype(BF16)
 
@@ -274,31 +256,37 @@
         lax.fori_loop(0, 4, body, 0)
 
     halves = (core, 1 - core)
-    swap(0)
     swap(1)
-    strip(images[0], core)
-    onward(0)
-    c_got = second(c_view, every, c_got)
     swap(2)
     strip(images[1], core)
-    onward(1)
     swap(3)
+    swaps[1].wait_recv()
+    onward(1, 0)
+    c_got = second(c_view, every, c_got)
     strip(images[2], core)
+    swaps[2].wait_recv()
+    onward(2, 0)
     strip(images[3], core)
-    onward(2)
+    swaps[3].wait_recv()
+    onward(3, 0)
+    swap(0)
+    for k in (1, 2, 3):
+        links.sent(z_sent[k, 0])
+        onward(k, 1)
+    strip(images[0], core)
+    swaps[0].wait_recv()
+    joined(0)
+    h2 = links.make(act.at[core], hcross, cross)
+
+    @pl.when(has_cross)
+    def _():
+        h2.start()
+
     received(c_got)
     whole = call_.at[core]
     c_swap = links.start(whole, whole, sibling)
-    swaps[3].wait_recv()
-    joined(core)
-    h2 = links.make(act.at[core], hcross, cross)
-
-    @pl.when(has_cross)
-    def _():
-        h2.start()
-
     unpack(core)
-    joined(1 - core)
+    joined(1)
     h1 = links.start(act.at[1 - core], hsib, sibling)
     c_swap.wait_recv()
     unpack(1 - core)
@@ -370,6 +358,7 @@
             pltpu.VMEM((4, 512, 256), BF16),
             pltpu.VMEM((4, 1, 256), F32),
             pltpu.VMEM((128, 512), F32),
+            pltpu.VMEM((512, 128), F32),
             pltpu.VMEM((128, 128), F32),
             pltpu.VMEM((32, 128), BF16),
             pltpu.VMEM((8, 32, 128), BF16),
@@ -381,8 +370,8 @@
             pltpu.VMEM((128, 128), F32),
             pltpu.VMEM((4, 2, 256, 256), BF16),
             pltpu.VMEM((4, 256, 256), BF16),
-            pltpu.VMEM((3, 2, 128, 256), BF16),
-            pltpu.VMEM((5, 2, 128, 256), BF16),
+            pltpu.VMEM((4, 2, 128, 256), BF16),
+            pltpu.VMEM((4, 2, 128, 256), BF16),
             pltpu.VMEM((2, 128, 256), BF16),
             pltpu.VMEM((128, 256), BF16),
             pltpu.VMEM((128, 256), BF16),
@@ -394,7 +383,6 @@
             pltpu.SemaphoreType.DMA((TAPS,)),
             pltpu.SemaphoreType.DMA((N_COPIES,)),
             pltpu.SemaphoreType.DMA((N_COPIES,)),
-            pltpu.SemaphoreType.DMA((5, 2)),
         ],
         compiler_params=pltpu.CompilerParams(
             collective_id=0, has_side_effects=True, vmem_limit_bytes=56 * 1024 * 1024

time: 55.2 us -> 53.3 us (0.966)
  Pallas kernels: 53.3 us -> 51.5 us
    pallas_call x1, Pallas kernels: 53.3 us -> 51.5 us  [per_device(): pl.pallas_call(kernel, out_shape=jax.ShapeDtypeStruct((8, 128, 64), BF16)...]
where the time goes in v4:
time: 53.3 us; the launch traced here: 53.1 us
  Pallas kernels  51.5 us (97%)
  local copies, waits for them, and re-layouts  1.67 us (3%)
    pallas_call x1, Pallas kernels, per_device(): pl.pallas_call(kernel, out_shape=jax.ShapeDtypeStruct((8, 128, 64), BF16)...  51.5 us
    unnamed x1, local copies, waits for them, and re-layouts  1.67 us

profile of v4, /device:TPU:1, one launch (start us, length us, event | category | flops | bytes accessed | tf_op | source)
XLA Modules:
  0.0 53.1 jit_solution(9735984268488606549)
XLA Ops:
  0.0 51.5 %shard_map.55 = bf16[8,128,64]{2,1,0:T(8,128)(2,1)} custom-call(bf16[4,2048,512]{2,1,0:T(8,128)(2,1)} %bitcast.6, f32[4,512]{1,0:T(4,128)} %gain_ref.1, bf16[4,16,256]{2,1,0:T(8,128)(2,1)} %w_ref.1, bf16[72,256]{1,0:T(8,128)(2,1)} %c1_ref.1, bf16[32,72]{1,0:T(8,128)(2,1)} %bitcast.7), custom_call_target="tpu_custom_call" | custom-call | flops 4000000000 | bytes 10000000 | tf_op jit(solution)/shard_map/pallas_call | solution.py:349
  51.5 1.7 %copy.7 = bf16[4,8,64,32]{2,3,1,0:T(8,128)(2,1)} copy(bf16[4,8,64,32]{2,3,1,0:T(8,128)(2,1)} %bitcast.5) | data formatting | bytes 262144

commit v5 on v4

--- a/solution.py
+++ b/solution.py
@@ -91,6 +91,11 @@
 
     every = slice(None)
 
+    def everyone(refs):
+        copies = {k: links.start(*refs(k), peers[k - 1]) for k in (4, 3, 5, 2, 6, 1, 7)}
+        return [copies[k] for k in range(1, 8)]
+
+
     def w_view(half, xi, yi, zi):
         return wall.at[2 * half : 2 * half + 2, xi, zi, yi]
 
@@ -149,7 +154,7 @@
     w_near = second(w_view, zhi, w_near)
     total = stats(3, total)
     tot[...] = total.T.reshape(8, 16, 128)
-    sent = [links.start(tot.at[(sec + k) % 8], tparts.at[k], peers[k - 1]) for k in range(1, 8)]
+    sent = everyone(lambda k: (tot.at[(sec + k) % 8], tparts.at[k]))
 
     received(c2_got)
     c2all[0] = c2pad[...]
@@ -182,7 +187,7 @@
         outs += [r, r * mean]
     tall[sec] = jnp.concatenate(outs, axis=0)
     mine = tall.at[sec]
-    sent = [links.start(mine, mine, peers[k - 1]) for k in range(1, 8)]
+    sent = everyone(lambda k: (mine, mine))
 
     def scale(zi):
         for t in range(TAPS):
@@ -311,7 +316,7 @@
     def finished(which_half, p):
         total = convolved(x2, 1, 128 * which_half, 128) + res[which_half]
         packed[p] = total.T.astype(BF16).reshape(8, 32, 128)
-        return [links.start(packed.at[p, (sec + k) % 8], arrived.at[p, k], peers[k - 1]) for k in range(1, 8)]
+        return everyone(lambda k: (packed.at[p, (sec + k) % 8], arrived.at[p, k]))
 
     columns(jnp.maximum(res[...].reshape(256, 256), 0.0), x1, 128)
     h1.wait_recv()
@@ -333,7 +338,7 @@
 
     for p in range(2):
         arrived[p, 0] = packed[p, sec]
-        for k in range(8):
+        for k in (0, 1, 7, 2, 6, 3, 5, 4):
             if k:
                 outs[p][k - 1].wait_recv()
             their = (core + k) % 2

time: 53.3 us -> 53.5 us (level)
  no operation moved by 1% of the time
where the time goes in v5:
time: 53.5 us; the launch traced here: 53 us
  Pallas kernels  51.4 us (96%)
  local copies, waits for them, and re-layouts  1.67 us (3%)
    pallas_call x1, Pallas kernels, per_device(): pl.pallas_call(kernel, out_shape=jax.ShapeDtypeStruct((8, 128, 64), BF16)...  51.4 us
    unnamed x1, local copies, waits for them, and re-layouts  1.67 us

profile of v5, /device:TPU:1, one launch (start us, length us, event | category | flops | bytes accessed | tf_op | source)
XLA Modules:
  0.0 53.0 jit_solution(13622726386511712734)
XLA Ops:
  0.0 51.4 %shard_map.55 = bf16[8,128,64]{2,1,0:T(8,128)(2,1)} custom-call(bf16[4,2048,512]{2,1,0:T(8,128)(2,1)} %bitcast.6, f32[4,512]{1,0:T(4,128)} %gain_ref.1, bf16[4,16,256]{2,1,0:T(8,128)(2,1)} %w_ref.1, bf16[72,256]{1,0:T(8,128)(2,1)} %c1_ref.1, bf16[32,72]{1,0:T(8,128)(2,1)} %bitcast.7), custom_call_target="tpu_custom_call" | custom-call | flops 4000000000 | bytes 10000000 | tf_op jit(solution)/shard_map/pallas_call | solution.py:354
  51.4 1.7 %copy.7 = bf16[4,8,64,32]{2,3,1,0:T(8,128)(2,1)} copy(bf16[4,8,64,32]{2,3,1,0:T(8,128)(2,1)} %bitcast.5) | data formatting | bytes 262144
